TPU v7x, 32 devices: a whole 2x2x4 slice. The times are simulated.
32 devices in a mesh: dp: 4 (over y, core), mp: 8 (over z, x).
Axes of the slice: x: 2, y: 2, z: 4, core: 2. Of those that a mesh axis runs over, the one named last changes fastest.
Arguments:
- embed_table: float32 [131072, 128], P(('dp', 'mp')), may hold values from -4 to 4
- dual_state: float32 [131072, 128], P(('dp', 'mp')), may hold values from -6 to 6
- grad_squares: float32 [131072, 128], P(('dp', 'mp')), may hold values from 0.002 to 0.2
- indices_now: int32 [2048, 16], P('dp', 'mp'), may hold values from 0 to 131071, as said below
- indices_next: int32 [2048, 16], P('dp', 'mp'), may hold values from 0 to 131071, as said below
- click_labels: int32 [2048], P('dp'), may hold values 0 or 1
- first_weight: bfloat16 [2048, 1024], P('mp'), may hold values from -0.5 to 0.5
- first_bias: float32 [1024], replicated, may hold values from -6 to 6
- output_weight: float32 [1024], replicated, may hold values from -1 to 1
Outputs:
- updated_table: float32 [131072, 128], P(('dp', 'mp'))
- updated_dual: float32 [131072, 128], P(('dp', 'mp'))
- updated_squares: float32 [131072, 128], P(('dp', 'mp'))
- next_logits: float32 [2048], P('dp')
Inputs may be any that keep to these rules, and one draw needn't show every extreme that they name: `indices_now`: the row r is owned by device r // 4096 of dp+mp. The lookups of one device's block (its 512 samples and 2 fields) name at most 64 rows owned by any one device, counted with repeats, and exactly 64 for some owners in every block. `indices_next`: same law as indices_now: at most 64 lookups of one device's block go to rows of one owner, exactly 64 for some owners in every block.
All inputs are finite; a program needn't handle non-finite values. No bound on the sum of `click_labels` on one device may be relied on, other than what follows from the above.
Results may differ from a plain program's by a relative error of at most 0.015.
Values may be sent and summed in bfloat16 or wider, within the bound.
A program may use at most 64 MiB of HBM per device.

v0:
```python
import jax
import jax.numpy as jnp
from jax import lax
from jax.sharding import PartitionSpec as P

learn_alpha = 1.0
learn_beta = 1.0
lasso_weight = 0.1
ridge_weight = 0.1


def assign_slots(indices, rows_owned, devices, capacity):
    flat_ids = indices.reshape(-1)
    owners = flat_ids // rows_owned
    member = (owners[:, None] == jnp.arange(devices, dtype=jnp.int32)[None, :]).astype(jnp.int32)
    ranks = jnp.sum((jnp.cumsum(member, axis=0) - 1) * member, axis=1)
    slots = owners * capacity + ranks
    request = jnp.full((devices * capacity,), -1, jnp.int32).at[slots].set(flat_ids % rows_owned)
    return (slots, request.reshape(devices, capacity))


def send_requests(stacked):
    moved = lax.all_to_all(stacked, ("dp", "mp"), split_axis=0, concat_axis=0, tiled=True)
    return moved


def return_rows(fetched):
    moved = lax.all_to_all(fetched, ("dp", "mp"), split_axis=0, concat_axis=0, tiled=True)
    return moved


def send_grads(grads):
    moved = lax.all_to_all(
        grads.astype(jnp.bfloat16), ("dp", "mp"), split_axis=0, concat_axis=0, tiled=True
    ).astype(grads.dtype)
    return moved


def reduce_pre(partial_value, first_bias):
    summed_pre = lax.psum(partial_value.astype(jnp.bfloat16), "mp").astype(jnp.float32)
    return summed_pre + first_bias[None, :]


def logits_of(pre, output_weight):
    return jnp.dot(jax.nn.silu(pre), output_weight, precision=lax.Precision.HIGHEST)


def slope_of(pre, logits, labels, output_weight):
    error_term = jax.nn.sigmoid(logits) - labels.astype(jnp.float32)
    gate_value = jax.nn.sigmoid(pre)
    derivative = gate_value * (1.0 + pre * (1.0 - gate_value))
    return (error_term[:, None] * output_weight[None, :] * derivative).astype(jnp.bfloat16)


def proximal_update(weights, dual, squares, grads, touched):
    new_squares = squares + grads * grads
    sigma_term = (jnp.sqrt(new_squares) - jnp.sqrt(squares)) / learn_alpha
    new_dual = dual + grads - sigma_term * weights
    shrunk = new_dual - jnp.sign(new_dual) * lasso_weight
    scale_term = (learn_beta + jnp.sqrt(new_squares)) / learn_alpha + ridge_weight
    new_weights = jnp.where(
        jnp.abs(new_dual) <= lasso_weight, jnp.zeros_like(shrunk), -shrunk / scale_term
    )
    keep = touched[:, None]
    return (
        jnp.where(keep, new_weights, weights),
        jnp.where(keep, new_dual, dual),
        jnp.where(keep, new_squares, squares),
    )


def shards(
    embed_table,
    dual_state,
    grad_squares,
    indices_now,
    indices_next,
    click_labels,
    first_weight,
    first_bias,
    output_weight,
):
    data_count = lax.axis_size("dp")
    model_count = lax.axis_size("mp")
    devices = data_count * model_count
    rows_owned = embed_table.shape[0]
    row_width = embed_table.shape[1]
    samples = indices_now.shape[0]
    field_columns = first_weight.shape[0]
    capacity = 2 * indices_now.size // devices
    slots_now, request_now = assign_slots(indices_now, rows_owned, devices, capacity)
    slots_next, request_next = assign_slots(indices_next, rows_owned, devices, capacity)
    asked = send_requests(jnp.stack((request_now, request_next), axis=1))
    asked_now = asked[:, 0].reshape(-1)
    asked_next = asked[:, 1].reshape(-1)
    valid_now = asked_now >= 0
    safe_now = jnp.maximum(asked_now, 0)
    safe_next = jnp.maximum(asked_next, 0)
    fetched_now = embed_table[safe_now].astype(jnp.bfloat16).reshape(devices, capacity, row_width)
    returned_now = return_rows(fetched_now).reshape(devices * capacity, row_width)
    looked_now = returned_now[slots_now].reshape(samples, field_columns)
    partial_now = jnp.dot(looked_now, first_weight, preferred_element_type=jnp.float32)
    pre_now = reduce_pre(partial_now, first_bias)
    logits_now = logits_of(pre_now, output_weight)
    slope = slope_of(pre_now, logits_now, click_labels, output_weight)
    row_grads = lax.dot_general(
        slope, first_weight, (((1,), (1,)), ((), ())), preferred_element_type=jnp.float32
    )
    outgoing = (
        jnp.zeros((devices * capacity, row_width), jnp.float32)
        .at[slots_now]
        .set(row_grads.reshape(-1, row_width))
    )
    arrived = send_grads(outgoing.reshape(devices, capacity, row_width)).reshape(
        devices * capacity, row_width
    )
    masked = jnp.where(valid_now[:, None], arrived, jnp.zeros_like(arrived))
    summed = jnp.zeros(embed_table.shape, jnp.float32).at[safe_now].add(masked)
    hits = jnp.zeros((rows_owned,), jnp.int32).at[safe_now].add(valid_now.astype(jnp.int32))
    updated_table, updated_dual, updated_squares = proximal_update(
        embed_table, dual_state, grad_squares, summed, hits > 0
    )
    fetched_next = (
        updated_table[safe_next].astype(jnp.bfloat16).reshape(devices, capacity, row_width)
    )
    returned_next = return_rows(fetched_next).reshape(devices * capacity, row_width)
    looked_next = returned_next[slots_next].reshape(samples, field_columns)
    partial_next = jnp.dot(looked_next, first_weight, preferred_element_type=jnp.float32)
    pre_next = reduce_pre(partial_next, first_bias)
    logits_part = logits_of(pre_next, output_weight)
    return (updated_table, updated_dual, updated_squares, logits_part)


def solution(mesh):
    placed = (
        P(("dp", "mp"), None),
        P(("dp", "mp"), None),
        P(("dp", "mp"), None),
        P("dp", "mp"),
        P("dp", "mp"),
        P("dp"),
        P("mp", None),
        P(),
        P(),
    )
    return jax.shard_map(
        shards,
        mesh=mesh,
        in_specs=placed,
        out_specs=(P(("dp", "mp"), None), P(("dp", "mp"), None), P(("dp", "mp"), None), P("dp")),
        check_vma=False,
    )
```

profile of v0, /device:TPU:0, one launch (start us, length us, event | category | flops | bytes accessed | tf_op | source)
XLA Modules:
  0.0 335.7 jit_solution(8298012784126590127)
XLA Ops:
  7.2 0.9 copy.23
  8.6 1.0 copy.28
  10.2 9.0 %reduce-window.14 = s32[32,8,128]{2,1,0:T(8,128)S(1)} reduce-window(s32[32,8,128]{2,1,0:T(8,128)S(1)} %fusion.27, s32[]{:T(128)} %constant.63.clone.1), window={size=1x1x128 pad=0_0x0_0x127_0}, to_apply=%region_0.1 | reduce-window | flops 4161536 | bytes 262148 | tf_op jit(solution)/shard_map/reduce-window
  19.7 4.3 %scatter_custom_fusion = s32[2048]{0:T(1024)S(1)} fusion(s32[1024]{0:T(1024)S(1)} %bitcast.65, s32[1024]{0:T(1024)S(1)} %get-tuple-element.9, s32[]{:T(128)} %constant.64.clone.1), kind=kCustom, calls=%fused_computation.102 | custom fusion | bytes 8196 | tf_op jit(solution)/shard_map/scatter | solution.py:18
  24.2 9.0 %reduce-window.16 = s32[32,8,128]{2,1,0:T(8,128)S(1)} reduce-window(s32[32,8,128]{2,1,0:T(8,128)S(1)} %fusion.28, s32[]{:T(128)} %constant.63.clone.1), window={size=1x1x128 pad=0_0x0_0x127_0}, to_apply=%region_4.5 | reduce-window | flops 4161536 | bytes 262148 | tf_op jit(solution)/shard_map/reduce-window.2
  33.7 4.3 %scatter_custom_fusion.1 = s32[2048]{0:T(1024)S(1)} fusion(s32[1024]{0:T(1024)S(1)} %bitcast.63, s32[1024]{0:T(1024)S(1)} %get-tuple-element.11, s32[]{:T(128)} %constant.64.clone.1), kind=kCustom, calls=%fused_computation.100 | custom fusion | bytes 8196 | tf_op jit(solution)/shard_map/scatter | solution.py:18
  38.3 14.2 %all_to_all.20 = s32[32,1,128]{2,1,0:T(1,128)S(1)} all-to-all(s32[32,1,128]{2,1,0:T(1,128)S(1)} %reshape.446), channel_id=1, replica_groups=mesh['dp'=4,'mp'=8] {'dp','mp'}, dimensions={0} | all-to-all | bytes 32768 | tf_op jit(solution)/shard_map/all_to_all | solution.py:23
  52.5 0.5 broadcast.396
  53.0 0.7 reduce.10
  54.0 7.7 %gather_fusion = bf16[2048,128]{1,0:T(8,128)(2,1)} fusion(f32[4096,128]{1,0:T(8,128)S(1)} %copy-done.1, s32[2048]{0:T(1024)S(1)} %broadcast_clamp_fusion.1), kind=kCustom, calls=%fused_computation | custom fusion | bytes 1056768 | tf_op jit(solution)/shard_map/gather | solution.py:99
  61.7 2.6 all-to-all-start.1
  64.4 16.3 %all-to-all-done.1 = bf16[32,64,128]{2,1,0:T(8,128)(2,1)S(1)} async-done(((bf16[32,64,128]{2,1,0:T(8,128)(2,1)}), bf16[32,64,128]{2,1,0:T(8,128)(2,1)S(1)}, u32[]{:S(2)}, u32[]{:S(2)}) %all-to-all-start.1) | async-done | bytes 524320 | tf_op jit(solution)/shard_map/all_to_all | solution.py:28
  80.6 3.2 gather_fusion.1
  84.0 1.4 convolution_convert_fusion.1
  85.4 75.8 %all-reduce.3.cloned.1.call-done = bf16[512,1024]{1,0:T(8,128)(2,1)} async-done(((bf16[512,1024]{1,0:T(8,128)(2,1)}), bf16[512,1024]{1,0:T(8,128)(2,1)}) %all-reduce.3.cloned.1.call-update) | async-done | bytes 1048592 | tf_op jit(solution)/shard_map/psum | solution.py:40
  161.2 3.6 %fusion.8 = f32[1,512]{1,0:T(1,128)S(1)} fusion(f32[1024,1]{0,1:T(1,128)S(1)} %bitcast.69, bf16[512,1024]{1,0:T(8,128)(2,1)} %all-reduce.3.cloned.1.call-done, f32[1024]{0:T(1024)S(1)} %copy-done.5), kind=kOutput, calls=%fused_computation.22 | convolution fusion | flops 9437184 | bytes 1058816 | tf_op jit(solution)/shard_map/dot_general | solution.py:45
  164.9 1.0 fusion.18
  166.0 0.8 reshape.403
  166.8 4.5 %scatter_custom_fusion.3 = f32[2048,128]{1,0:T(8,128)} fusion(s32[1024]{0:T(1024)S(1)} %bitcast.67, f32[1024,128]{1,0:T(8,128)} %reshape.403, f32[]{:T(128)} %constant.71.clone.1), kind=kCustom, calls=%fused_computation.39 | custom fusion | bytes 1049088 | tf_op jit(solution)/shard_map/scatter | solution.py:112
  171.3 2.1 convert_element_type.61
  173.3 4.2 %all-to-all-start.2 = ((bf16[32,64,128]{2,1,0:T(8,128)(2,1)}), bf16[32,64,128]{2,1,0:T(8,128)(2,1)S(1)}, u32[]{:S(2)}, u32[]{:S(2)}) async-start(bf16[32,64,128]{2,1,0:T(8,128)(2,1)} %bitcast.12), calls=%async_computation.2 | async-start | bytes 1048576 | tf_op jit(solution)/shard_map/all_to_all | solution.py:33
  177.8 11.4 %scatter_custom_fusion.2 = s32[4096]{0:T(1024)S(1)} fusion(s32[2048]{0:T(1024)S(1)} %reshape.393, s32[2048]{0:T(1024)S(1)} %convert_element_type.54, s32[]{:T(128)} %constant.63.clone.1), kind=kCustom, calls=%fused_computation.72 | custom fusion | flops 2048 | bytes 16388 | tf_op jit(solution)/shard_map/scatter-add | solution.py:119
  189.2 4.7 %all-to-all-done.2 = bf16[32,64,128]{2,1,0:T(8,128)(2,1)S(1)} async-done(((bf16[32,64,128]{2,1,0:T(8,128)(2,1)}), bf16[32,64,128]{2,1,0:T(8,128)(2,1)S(1)}, u32[]{:S(2)}, u32[]{:S(2)}) %all-to-all-start.2) | async-done | bytes 524320 | tf_op jit(solution)/shard_map/all_to_all | solution.py:33
  193.9 14.0 %scatter_custom_fusion.4 = f32[4096,128]{1,0:T(8,128)} fusion(s32[2048]{0:T(1024)S(1)} %reshape.393, bf16[2048,128]{1,0:T(8,128)(2,1)S(1)} %bitcast.56, f32[]{:T(128)} %constant.71.clone.1, pred[2048]{0:T(1024)(128)(4,1)S(1)} %ge.11), kind=kCustom, calls=%fused_computation.31 | custom fusion | flops 786432 | bytes 2624512 | tf_op jit(solution)/shard_map/scatter-add | solution.py:118
  207.9 6.2 %fusion.11 = (f32[4096,128]{1,0:T(8,128)}, f32[4096,128]{1,0:T(8,128)}, f32[4096,128]{1,0:T(8,128)}) fusion(f32[4096,128]{1,0:T(8,128)} %param.10, f32[4096,128]{1,0:T(8,128)S(1)} %copy-done.1, f32[4096,128]{1,0:T(8,128)} %param.11, f32[4096,128]{1,0:T(8,128)} %scatter_custom_fusion.4, pred[4096]{0:T(1024)(128)(4,1)S(1)} %broadcast_compare_fusion), kind=kLoop, calls=%fused_computation.27 | loop fusion | flops 9437184 | bytes 14684160 | tf_op jit(solution)/shard_map/jit(_where)/select_n | solution.py:67
  214.1 9.2 %gather_fusion.2 = bf16[2048,128]{1,0:T(8,128)(2,1)} fusion(f32[4096,128]{1,0:T(8,128)} %get-tuple-element.7, s32[2048]{0:T(1024)S(1)} %broadcast_clamp_fusion), kind=kCustom, calls=%fused_computation.2 | custom fusion | bytes 1056768 | tf_op jit(solution)/shard_map/gather | solution.py:124
  223.4 4.4 %all-to-all-start.3 = ((bf16[32,64,128]{2,1,0:T(8,128)(2,1)}), bf16[32,64,128]{2,1,0:T(8,128)(2,1)S(1)}, u32[]{:S(2)}, u32[]{:S(2)}) async-start(bf16[32,64,128]{2,1,0:T(8,128)(2,1)} %bitcast.14), calls=%async_computation.3 | async-start | bytes 1048576 | tf_op jit(solution)/shard_map/all_to_all | solution.py:28
  227.9 16.3 %all-to-all-done.3 = bf16[32,64,128]{2,1,0:T(8,128)(2,1)S(1)} async-done(((bf16[32,64,128]{2,1,0:T(8,128)(2,1)}), bf16[32,64,128]{2,1,0:T(8,128)(2,1)S(1)}, u32[]{:S(2)}, u32[]{:S(2)}) %all-to-all-start.3) | async-done | bytes 524320 | tf_op jit(solution)/shard_map/all_to_all | solution.py:28
  244.1 3.2 gather_fusion.3
  247.5 1.5 convolution_convert_fusion
  249.0 75.8 %all-reduce.5.cloned.1.call-done = bf16[512,1024]{1,0:T(8,128)(2,1)} async-done(((bf16[512,1024]{1,0:T(8,128)(2,1)}), bf16[512,1024]{1,0:T(8,128)(2,1)}) %all-reduce.5.cloned.1.call-update) | async-done | bytes 1048592 | tf_op jit(solution)/shard_map/psum | solution.py:40
  324.7 4.1 %fusion = f32[1,512]{1,0:T(1,128)} fusion(f32[1024,1]{0,1:T(1,128)S(1)} %bitcast.70, bf16[512,1024]{1,0:T(8,128)(2,1)} %all-reduce.5.cloned.1.call-done, f32[1024]{0:T(1024)S(1)} %copy-done.5), kind=kOutput, calls=%fused_computation.9 | convolution fusion | flops 9437184 | bytes 1058816 | tf_op jit(solution)/shard_map/dot_general | solution.py:45
  (63 shorter events, 3.3 us)
Async XLA Ops:
  7.2 76.8 %copy-start = (bf16[256,1024]{1,0:T(8,128)(2,1)S(1)}, bf16[256,1024]{1,0:T(8,128)(2,1)}, u32[]{:S(2)}) copy-start(bf16[256,1024]{1,0:T(8,128)(2,1)} %param.15) | copy-start | bytes 1572868
  8.6 45.4 %copy-start.1 = (f32[4096,128]{1,0:T(8,128)S(1)}, f32[4096,128]{1,0:T(8,128)}, u32[]{:S(2)}) copy-start(f32[4096,128]{1,0:T(8,128)} %param.9) | copy-start | bytes 6291460
  61.7 19.0 %all-to-all-start.1 = ((bf16[32,64,128]{2,1,0:T(8,128)(2,1)}), bf16[32,64,128]{2,1,0:T(8,128)(2,1)S(1)}, u32[]{:S(2)}, u32[]{:S(2)}) async-start(bf16[32,64,128]{2,1,0:T(8,128)(2,1)} %bitcast.55), calls=%async_computation.1 | async-start | bytes 1048576 | tf_op jit(solution)/shard_map/all_to_all | solution.py:28
  64.3 96.9 %all-reduce.3.cloned.1.call-start = ((), (), s32[]{:S(2)}) async-start(), calls=%async_computation.4 | async-start | bytes 2097152 | tf_op jit(solution)/shard_map/psum | solution.py:40
  83.9 77.4 %copy-start.4 = (f32[1024]{0:T(1024)S(1)}, f32[1024]{0:T(1024)}, u32[]{:S(2)}) copy-start(f32[1024]{0:T(1024)} %param.17) | copy-start | bytes 12292
  83.9 77.4 %copy-start.5 = (f32[1024]{0:T(1024)S(1)}, f32[1024]{0:T(1024)}, u32[]{:S(2)}) copy-start(f32[1024]{0:T(1024)} %param.16) | copy-start | bytes 12292
  161.2 3.6 %copy-start.2 = (s32[512]{0:T(512)S(1)}, s32[512]{0:T(512)}, u32[]{:S(2)}) copy-start(s32[512]{0:T(512)} %param.14) | copy-start | bytes 6148
  161.2 3.7 %copy-start.3 = (bf16[512,1024]{1,0:T(8,128)(2,1)S(1)}, bf16[512,1024]{1,0:T(8,128)(2,1)}, u32[]{:S(2)}) copy-start(bf16[512,1024]{1,0:T(8,128)(2,1)} %all-reduce.3.cloned.1.call-done) | copy-start | bytes 3145732
  173.3 20.6 %all-to-all-start.2 = ((bf16[32,64,128]{2,1,0:T(8,128)(2,1)}), bf16[32,64,128]{2,1,0:T(8,128)(2,1)S(1)}, u32[]{:S(2)}, u32[]{:S(2)}) async-start(bf16[32,64,128]{2,1,0:T(8,128)(2,1)} %bitcast.12), calls=%async_computation.2 | async-start | bytes 1048576 | tf_op jit(solution)/shard_map/all_to_all | solution.py:33
  223.4 20.8 %all-to-all-start.3 = ((bf16[32,64,128]{2,1,0:T(8,128)(2,1)}), bf16[32,64,128]{2,1,0:T(8,128)(2,1)S(1)}, u32[]{:S(2)}, u32[]{:S(2)}) async-start(bf16[32,64,128]{2,1,0:T(8,128)(2,1)} %bitcast.14), calls=%async_computation.3 | async-start | bytes 1048576 | tf_op jit(solution)/shard_map/all_to_all | solution.py:28
  227.8 96.9 %all-reduce.5.cloned.1.call-start = ((), (), s32[]{:S(2)}) async-start(), calls=%async_computation.5 | async-start | bytes 2097152 | tf_op jit(solution)/shard_map/psum | solution.py:40
Sparse Core Ops, SparseCore 0:
  85.5 75.6 all-reduce.2
  249.1 75.6 all-reduce.4
where the time goes:
time: 336 us
  waiting for transfers between devices  189 us (56%)
  other arithmetic  53.2 us (16%)
  local copies, waits for them, and re-layouts  42 us (12%)
  between operations  14.4 us (4%)
  blocking collectives  14.2 us (4%)
  matrix products  11.7 us (3%)
  starting transfers between devices  11.3 us (3%)
    psum x2, waiting for transfers between devices, reduce_pre(): lax.psum(partial_value.astype(jnp.bfloat16), 'mp').astype(jnp.float32)  152 us
    all_to_all x2, waiting for transfers between devices, return_rows(): lax.all_to_all(fetched, ('dp', 'mp'), split_axis=0, concat_axis=0, tiled=...  32.6 us
    another operation x4, other arithmetic  18.1 us
    all_to_all x1, blocking collectives, send_requests(): lax.all_to_all(stacked, ('dp', 'mp'), split_axis=0, concat_axis=0, tiled=...  14.2 us
    scatter-add x1, other arithmetic, shards(): summed = jnp.zeros(embed_table.shape, jnp.float32).at[safe_now].add(masked)  14 us
    scatter-add x1, other arithmetic, shards(): jnp.zeros((rows_owned,), jnp.int32).at[safe_now]  11.4 us
    gather x1, local copies, waits for them, and re-layouts, shards(): updated_table[safe_next].astype(jnp.bfloat16)  9.21 us
    scatter x2, local copies, waits for them, and re-layouts, assign_slots(): jnp.full((devices * capacity,), -1, jnp.int32).at[slots]  8.63 us
  transfers between devices with their start and end apart: 5, of which 5 were waited for; matrix products, arithmetic and copies ran while one was open for 3% of the time, Pallas kernels for 0%

commit v1 on v0

v1 whole, which is shorter than its diff:
```python
import functools

import jax
import jax.numpy as jnp
from jax import lax
from jax.experimental import pallas as pl
from jax.experimental.pallas import tpu as pltpu
from jax.sharding import PartitionSpec as P

MESH = pl.DeviceIdType.MESH
LASSO = 0.1
RIDGE = 0.1
BETA = 1.0
F32 = jnp.float32
BF16 = jnp.bfloat16


def onehot(mask):
    return jnp.where(mask, 1.0, 0.0).astype(BF16)


def mm(a, b):
    return jnp.dot(a, b, preferred_element_type=F32)


def log2(v):
    assert v & (v - 1) == 0
    return v.bit_length() - 1


def train(
    D, M, C, GROUP,
    cols, labels, bias, wout, table_h, dual_h, sq_h, w_h,
    tab_o, dual_o, sq_o, lg_o,
    tab, dual, sq, tabh, newh, w,
    rowscr, req_send, asked, idcol, idrow,
    send_now, recv_now, send_grad, recv_grad, send_next, recv_next,
    look, part_send, part_recv, slope, rg, rg_out, lg_all,
    lsem, osem, ssem, rsem,
):
    S = cols.shape[0]
    F = cols.shape[1] // 2
    R, W = tab.shape
    H = bias.shape[1]
    FW = F * W
    half = S // 2
    nb = M // 2
    B = half // nb
    slots = D * C
    rsh, csh = log2(R), log2(C)
    dp, mp = lax.axis_index("dp"), lax.axis_index("mp")
    me = dp * M + mp
    h = lax.rem(mp, 2)
    myb = lax.div(mp, 2)
    partner = (dp, mp + 1 - 2 * h)

    def device(p):
        return (lax.div(p, M), lax.rem(p, M))

    bar = pltpu.get_barrier_semaphore()

    def greet(k, c):
        pl.semaphore_signal(
            bar, inc=1, device_id=device(lax.rem(me + k, D)), device_id_type=MESH
        )
        return c

    lax.fori_loop(1, D, greet, 0)

    loads = [
        pltpu.make_async_copy(table_h, tab, lsem.at[0]),
        pltpu.make_async_copy(w_h, w.at[0], lsem.at[1]),
        pltpu.make_async_copy(dual_h, dual, lsem.at[2]),
        pltpu.make_async_copy(sq_h, sq, lsem.at[3]),
    ]
    for load in loads:
        load.start()

    def remote(src, dst, n, to):
        return pltpu.make_async_remote_copy(
            src_ref=src, dst_ref=dst, send_sem=ssem.at[n], recv_sem=rsem.at[n],
            device_id=to, device_id_type=MESH,
        )

    lane = lax.broadcasted_iota(jnp.int32, (S, 128), 1)
    tri = onehot(
        lax.broadcasted_iota(jnp.int32, (S, S), 0)
        > lax.broadcasted_iota(jnp.int32, (S, S), 1)
    )
    owners, members = [], []
    for q in range(2 * F):
        owner = (lax.shift_right_logical(cols[:, q : q + 1], rsh) - me) & (D - 1)
        owners.append(owner)
        members.append(jnp.where(owner == lane, 1.0, 0.0))
    counts = mm(tri, jnp.concatenate(members, axis=1).astype(BF16))
    ranks = []
    packed = jnp.zeros((S, 128), F32)
    for q in range(2 * F):
        count = counts[:, q * 128 : (q + 1) * 128]
        for before in range((q // F) * F, q):
            count = count + jnp.sum(members[before], axis=0, keepdims=True)
        rank = jnp.sum(count * members[q], axis=1, keepdims=True).astype(jnp.int32)
        ranks.append(rank)
        packed = jnp.where(lane == q, (owners[q] * C + rank).astype(F32), packed)
    rowscr[...] = packed.T[0:8, :].astype(jnp.int32)
    total = jnp.zeros((D, 256), F32)
    owner_iota = lax.broadcasted_iota(jnp.int32, (D, S), 0)
    for q in range(2 * F):
        owner_row = lax.shift_right_logical(rowscr[q : q + 1, :], csh)
        which = ranks[q] + (q // F) * C == lane
        value = (cols[:, q : q + 1] & (R - 1)) + 1
        high = jnp.where(which, lax.shift_right_logical(value, 6).astype(F32), 0.0)
        low = jnp.where(which, (value & 63).astype(F32), 0.0)
        total += mm(
            onehot(owner_row == owner_iota),
            jnp.concatenate([high, low], axis=1).astype(BF16),
        )
    request = (total[:, :128] * 64.0 + total[:, 128:]).astype(jnp.int32) - 1
    for r in range(D):
        req_send[r * 8 : (r + 1) * 8, :] = jnp.broadcast_to(request[r : r + 1, :], (8, 128))

    pl.semaphore_wait(bar, D - 1)

    def exchange(rows, send, recv, n, first, last):
        def one(r, c):
            remote(
                send.at[pl.ds(pl.multiple_of(r * rows, rows), rows)],
                recv.at[pl.ds(pl.multiple_of((D - r) * rows, rows), rows)],
                n, device(lax.rem(me + r, D)),
            ).start()
            return c

        lax.fori_loop(first, last, one, 0)

    def arrived(rows, send, recv, n):
        area = pl.ds(rows, (D - 1) * rows)
        return remote(send.at[area], recv.at[area], n, partner)

    exchange(8, req_send, asked, 0, 1, D)
    asked[0:8, :] = req_send[0:8, :]
    loads[1].wait()
    copy_w = remote(w.at[0], w.at[1], 1, partner)
    copy_w.start()
    loads[0].wait()
    tabh[...] = tab[...].astype(BF16)
    copy_req = arrived(8, req_send, asked, 0)
    copy_req.wait_recv()

    asked_t = asked[...].astype(F32).T.astype(jnp.int32)
    for r in range(D):
        for t in range(2):
            idcol[t, r * C : (r + 1) * C, :] = jnp.broadcast_to(
                asked_t[t * C : (t + 1) * C, 8 * r : 8 * r + 1], (C, 128)
            )

    KC = 1024

    def fetch(t, source, send, recv, n):
        def group(g, c):
            rows = pl.ds(pl.multiple_of(g * GROUP, GROUP), GROUP)
            ids = idcol[t, rows, 0:1]
            acc = jnp.zeros((GROUP, W), F32)
            for k in range(R // KC):
                pick = onehot(
                    ids == lax.broadcasted_iota(jnp.int32, (GROUP, KC), 1) + k * KC
                )
                acc = acc + mm(pick, source[k * KC : (k + 1) * KC, :])
            send[rows, :] = acc.astype(BF16)
            peers = GROUP // C
            exchange(C, send, recv, n, jnp.maximum(g * peers, 1), (g + 1) * peers)
            return c

        lax.fori_loop(0, slots // GROUP, group, 0)
        recv[0:C, :] = send[0:C, :]

    def forward(t, recv, n):
        for f in range(F):
            owner_rank = jnp.broadcast_to(slot_col[t * F + f], (S, slots))
            pick = onehot(owner_rank == lax.broadcasted_iota(jnp.int32, (S, slots), 1))
            got = mm(pick, recv[...]).astype(BF16)
            look[t, 0, :, f * W : (f + 1) * W] = got[:half]
            look[t, 1, :, f * W : (f + 1) * W] = got[half:]
        swap = remote(look.at[t, 1 - h], look.at[t, 2], n, partner)
        swap.start()
        if t == 0:
            copy_w.wait_recv()
        swap.wait_recv()

        def step(i, c):
            k = i + 1
            b = lax.rem(myb + k, nb)
            rows = pl.ds(pl.multiple_of(b * B, B), B)
            value = mm(look[t, h, rows, :], w[0]) + mm(look[t, 2, rows, :], w[1])
            part_send[t, k] = value.astype(BF16)
            remote(
                part_send.at[t, k], part_recv.at[t, nb - k], n + 1, (dp, 2 * b + h)
            ).start()
            return c

        lax.fori_loop(0, nb - 1, step, 0)
        rows = pl.ds(pl.multiple_of(myb * B, B), B)
        pre = mm(look[t, h, rows, :], w[0]) + mm(look[t, 2, rows, :], w[1])
        pre = pre + bias[...]
        moved = remote(
            part_send.at[t, pl.ds(1, nb - 1)], part_recv.at[t, pl.ds(1, nb - 1)],
            n + 1, partner,
        )
        moved.wait_recv()
        for k in range(1, nb):
            pre = pre + part_recv[t, k].astype(F32)
        gate = jax.nn.sigmoid(pre)
        logits = jnp.sum(pre * gate * wout[...], axis=1, keepdims=True)
        return pre, gate, logits, [swap, moved]

    slot_col = [owners[q] * C + ranks[q] for q in range(2 * F)]
    fetch(0, tabh, send_now, recv_now, 2)
    for blk in range(slots // 128):
        flipped = idcol[0, blk * 128 : (blk + 1) * 128, :].astype(F32).T
        idrow[:, blk * 128 : (blk + 1) * 128] = flipped[0:8, :].astype(jnp.int32)
    copy_now = arrived(C, send_now, recv_now, 2)
    copy_now.wait_recv()
    pre, gate, logits, sent_now = forward(0, recv_now, 3)
    mine = pl.ds(pl.multiple_of(h * half + myb * B, B), B)
    error = jax.nn.sigmoid(logits) - labels[mine, :].astype(F32)
    slope[0] = (error * wout[...] * (gate * (1.0 + pre * (1.0 - gate)))).astype(BF16)

    def spread(k, c):
        remote(
            slope.at[0], slope.at[nb - k], 5, (dp, 2 * lax.rem(myb + k, nb) + h)
        ).start()
        return c

    lax.fori_loop(1, nb, spread, 0)

    def back(k):
        rows = pl.ds(pl.multiple_of(lax.rem(myb + k, nb) * B, B), B)
        for side in range(2):
            value = lax.dot_general(
                slope[k], w[side], (((1,), (1,)), ((), ())), preferred_element_type=F32
            ).astype(BF16)
            if side == 0:
                rg[h, rows, :] = value
            else:
                rg_out[rows, :] = value

    back(0)
    copy_slope = remote(slope.at[pl.ds(1, nb - 1)], slope.at[pl.ds(1, nb - 1)], 5, partner)
    copy_slope.wait_recv()
    for k in range(1, nb):
        back(k)
    swap_grad = remote(rg_out, rg.at[h], 6, partner)
    swap_grad.start()
    swap_grad.wait_recv()

    def give(g, c):
        rows = pl.ds(pl.multiple_of(g * GROUP, GROUP), GROUP)
        acc = jnp.zeros((GROUP, W), F32)
        spot = lax.broadcasted_iota(jnp.int32, (GROUP, half), 0) + g * GROUP
        for f in range(F):
            for s in range(2):
                pick = onehot(rowscr[f : f + 1, s * half : (s + 1) * half] == spot)
                acc = acc + mm(pick, rg[s, :, f * W : (f + 1) * W])
        send_grad[rows, :] = acc.astype(BF16)
        peers = GROUP // C
        exchange(C, send_grad, recv_grad, 7, jnp.maximum(g * peers, 1), (g + 1) * peers)
        return c

    lax.fori_loop(0, slots // GROUP, give, 0)
    recv_grad[0:C, :] = send_grad[0:C, :]
    loads[2].wait()
    loads[3].wait()
    copy_grad = arrived(C, send_grad, recv_grad, 7)
    copy_grad.wait_recv()

    RC = 256
    gathered = jnp.concatenate([recv_grad[...], jnp.ones((slots, 128), BF16)], axis=1)

    def update(i, c):
        rows = pl.ds(pl.multiple_of(i * RC, RC), RC)
        spot = lax.broadcasted_iota(jnp.int32, (RC, slots), 0) + i * RC
        both = mm(onehot(idrow[0:1, :] == spot), gathered)
        g, keep = both[:, :W], both[:, W:] > 0.5
        old_w, old_d, old_s = tab[rows, :], dual[rows, :], sq[rows, :]
        new_s = old_s + g * g
        root = jnp.sqrt(new_s)
        new_d = old_d + g - (root - jnp.sqrt(old_s)) * old_w
        shrunk = jnp.where(new_d > 0.0, new_d - LASSO, new_d + LASSO)
        new_w = jnp.where(
            jnp.abs(new_d) <= LASSO, 0.0, -shrunk / ((BETA + root) + RIDGE)
        )
        new_w = jnp.where(keep, new_w, old_w)
        tab[rows, :] = new_w
        newh[rows, :] = new_w.astype(BF16)
        dual[rows, :] = jnp.where(keep, new_d, old_d)
        sq[rows, :] = jnp.where(keep, new_s, old_s)
        return c

    lax.fori_loop(0, R // RC, update, 0)
    stores = [
        pltpu.make_async_copy(tab, tab_o, osem.at[0]),
        pltpu.make_async_copy(dual, dual_o, osem.at[1]),
        pltpu.make_async_copy(sq, sq_o, osem.at[2]),
    ]
    for store in stores:
        store.start()

    fetch(1, newh, send_next, recv_next, 8)
    copy_next = arrived(C, send_next, recv_next, 8)
    copy_next.wait_recv()
    pre, gate, logits, sent_next = forward(1, recv_next, 9)
    wide = jnp.broadcast_to(logits, (B, 128))
    if B < 128:
        wide = jnp.concatenate([wide, jnp.zeros((128 - B, 128), F32)], axis=0)
    lg_all[mp] = wide.T[0:8, :]

    def tell(k, c):
        remote(lg_all.at[mp], lg_all.at[mp], 11, (dp, lax.rem(mp + k, M))).start()
        return c

    lax.fori_loop(1, M, tell, 0)
    for copy in (copy_req, copy_w, copy_now, *sent_now, copy_slope, swap_grad, copy_grad,
                 copy_next, *sent_next):
        copy.wait_send()
    for store in stores:
        store.wait()
    told = remote(lg_all.at[pl.ds(0, M - 1)], lg_all.at[pl.ds(0, M - 1)], 11, partner)
    told.wait_send()
    told.wait_recv()
    lg_o[...] = lg_all[...]


def shards(table, dual, squares, now, later, labels, weight, bias, wout):
    M = lax.axis_size("mp")
    D = lax.axis_size("dp") * M
    R, W = table.shape
    S, F = now.shape
    H = weight.shape[1]
    C = 2 * now.size // D
    slots = D * C
    GROUP = 512
    nb = M // 2
    B = S // M
    vm = pl.BlockSpec(memory_space=pltpu.VMEM)
    hb = pl.BlockSpec(memory_space=pl.ANY)
    rows_buf = pltpu.VMEM((slots, W), BF16)
    big = pltpu.VMEM((R, W), F32)
    state = jax.ShapeDtypeStruct((R, W), F32)
    outs = pl.pallas_call(
        functools.partial(train, D, M, C, GROUP),
        out_shape=(state, state, state, jax.ShapeDtypeStruct((M, 8, 128), F32)),
        in_specs=[vm, vm, vm, vm, hb, hb, hb, hb],
        out_specs=(hb, hb, hb, vm),
        scratch_shapes=[
            big, big, big,
            pltpu.VMEM((R, W), BF16), pltpu.VMEM((R, W), BF16),
            pltpu.VMEM((2, F * W, H), BF16),
            pltpu.VMEM((8, S), jnp.int32),
            pltpu.VMEM((D * 8, 128), jnp.int32), pltpu.VMEM((D * 8, 128), jnp.int32),
            pltpu.VMEM((2, slots, 128), jnp.int32), pltpu.VMEM((8, slots), jnp.int32),
            rows_buf, rows_buf, rows_buf, rows_buf, rows_buf, rows_buf,
            pltpu.VMEM((2, 3, S // 2, F * W), BF16),
            pltpu.VMEM((2, nb, B, H), BF16), pltpu.VMEM((2, nb, B, H), BF16),
            pltpu.VMEM((nb, B, H), BF16),
            pltpu.VMEM((2, S // 2, F * W), BF16), pltpu.VMEM((S // 2, F * W), BF16),
            pltpu.VMEM((M, 8, 128), F32),
            pltpu.SemaphoreType.DMA((4,)), pltpu.SemaphoreType.DMA((3,)),
            pltpu.SemaphoreType.DMA((12,)), pltpu.SemaphoreType.DMA((12,)),
        ],
        compiler_params=pltpu.CompilerParams(
            collective_id=0, has_side_effects=True, vmem_limit_bytes=58 * 1024 * 1024
        ),
    )(
        jnp.concatenate([now, later], axis=1), labels[:, None], bias[None, :],
        wout[None, :], table, dual, squares, weight,
    )
    logits = outs[3][:, 0, :B].reshape(nb, 2, B).transpose(1, 0, 2).reshape(S)
    return outs[0], outs[1], outs[2], logits


def solution(mesh):
    own = P(("dp", "mp"), None)
    placed = (own, own, own, P("dp", "mp"), P("dp", "mp"), P("dp"), P("mp", None), P(), P())
    return jax.shard_map(
        shards, mesh=mesh, in_specs=placed, out_specs=(own, own, own, P("dp")),
        check_vma=False,
    )
```

time: 336 us -> 138 us (0.41)
  waiting for transfers between devices: 189 us -> 0 us
  Pallas kernels: 0 us -> 125 us
  other arithmetic: 53.2 us -> 0.71 us
  local copies, waits for them, and re-layouts: 42 us -> 10.7 us
  blocking collectives: 14.2 us -> 0 us
  between operations: 14.4 us -> 0.65 us
  matrix products: 11.7 us -> 0 us
  starting transfers between devices: 11.3 us -> 0 us
    psum x2 -> x0, waiting for transfers between devices: 152 us -> none  [reduce_pre(): lax.psum(partial_value.astype(jnp.bfloat16), 'mp').astype(jnp.float32)]
    pallas_call x0 -> x1, Pallas kernels: none -> 125 us  [shards(): pl.pallas_call(functools.partial(train, D, M, C, GROUP), out_shape=(state...]
    all_to_all x3 -> x0, waiting for transfers between devices: 37.2 us -> none  [the longest x2 32.6 us: return_rows(): lax.all_to_all(fetched, ('dp', 'mp'), split_axis=0, concat_axis=0, tiled=...]
    scatter-add x2 -> x0, other arithmetic: 25.5 us -> none  [the longest x1 14 us: shards(): summed = jnp.zeros(embed_table.shape, jnp.float32).at[safe_now].add(masked)]
    gather x4 -> x0, local copies, waits for them, and re-layouts: 23.3 us -> none  [the longest x1 9.21 us: shards(): updated_table[safe_next].astype(jnp.bfloat16)]
    another operation x5 -> x0, other arithmetic: 18.1 us -> none
    all_to_all x1 -> x0, blocking collectives: 14.2 us -> none  [send_requests(): lax.all_to_all(stacked, ('dp', 'mp'), split_axis=0, concat_axis=0, tiled=...]
    scatter x3 -> x0, local copies, waits for them, and re-layouts: 13.1 us -> none  [the longest x2 8.63 us: assign_slots(): jnp.full((devices * capacity,), -1, jnp.int32).at[slots]]
  transfers between devices with their start and end apart: 5 -> 0, of which waited for: 5 -> 0; matrix products, arithmetic and copies ran while one was open for 3% -> 0% of each run, Pallas kernels for 0% -> 0%
where the time goes in v1:
time: 138 us; the launch traced here: 137 us
  Pallas kernels  125 us (91%)
  local copies, waits for them, and re-layouts  10.7 us (8%)
    pallas_call x1, Pallas kernels, shards(): pl.pallas_call(functools.partial(train, D, M, C, GROUP), out_shape=(state...  125 us
    unnamed x7, local copies, waits for them, and re-layouts  6.86 us

profile of v1, /device:TPU:0, one launch (start us, length us, event | category | flops | bytes accessed | tf_op | source)
XLA Modules:
  0.0 137.3 jit_solution(13787889015460391805)
XLA Ops:
  0.6 0.7 pad_add_fusion
  1.3 0.9 copy.19.cols
  2.2 1.5 %copy.20.labels = s32[512,1]{1,0:T(8,128)} copy(s32[512,1]{0,1:T(1,128)} %bitcast.11) | data formatting | bytes 4096 | tf_op jit(solution)/shard_map/broadcast_in_dim | solution.py:373
  3.7 125.3 %shard_map.120 = (f32[4096,128]{1,0:T(8,128)}, f32[4096,128]{1,0:T(8,128)}, f32[4096,128]{1,0:T(8,128)}, f32[8,8,128]{2,1,0:T(8,128)}) custom-call(s32[512,4]{1,0:T(8,128)} %copy.19.cols, s32[512,1]{1,0:T(8,128)} %copy.20.labels, f32[1,1024]{1,0:T(1,128)} %bitcast.9, f32[1,1024]{1,0:T(1,128)} %bitcast.10, f32[4096,128]{1,0:T(8,128)} %table_h.1, ...), custom_call_target="tpu_custom_call" | custom-call | tf_op jit(solution)/shard_map/pallas_call | solution.py:348
  129.0 0.8 slice.3
  129.8 0.7 reshape.11
  130.5 0.0 copy-start.1
  130.5 3.2 %copy.27 = f32[4096,128]{1,0:T(8,128)} copy(f32[4096,128]{1,0:T(8,128)} %get-tuple-element.16) | data formatting | bytes 4194304
  133.7 0.0 copy-done.1
  133.7 0.0 copy-start
  133.7 1.3 copy.28
  135.0 1.0 copy-done
  136.0 1.3 copy.29
  (1 shorter events, 0.0 us)
Async XLA Ops:
  130.5 3.2 %copy-start.1 = (f32[4096,128]{1,0:T(8,128)S(1)}, f32[4096,128]{1,0:T(8,128)}, u32[]{:S(2)}) copy-start(f32[4096,128]{1,0:T(8,128)} %get-tuple-element.17) | copy-start | bytes 6291460
  133.7 2.3 %copy-start = (f32[4096,128]{1,0:T(8,128)S(1)}, f32[4096,128]{1,0:T(8,128)}, u32[]{:S(2)}) copy-start(f32[4096,128]{1,0:T(8,128)} %get-tuple-element.18) | copy-start | bytes 6291460

commit v2 on v1

--- a/solution.py
+++ b/solution.py
@@ -11,6 +11,7 @@
 LASSO = 0.1
 RIDGE = 0.1
 BETA = 1.0
+TEAM = 4
 F32 = jnp.float32
 BF16 = jnp.bfloat16
 
@@ -30,29 +31,37 @@
 
 def train(
     D, M, C, GROUP,
-    cols, labels, bias, wout, table_h, dual_h, sq_h, w_h,
+    now_t, later_t, labels_t, bias, wout, table_h, dual_h, sq_h, w_h,
     tab_o, dual_o, sq_o, lg_o,
-    tab, dual, sq, tabh, newh, w,
-    rowscr, req_send, asked, idcol, idrow,
+    tab, dual, sq, tabh, newh, w, scatter,
+    colscr, slotcol, rowscr, req_send, asked, idcol, idrow,
     send_now, recv_now, send_grad, recv_grad, send_next, recv_next,
-    look, part_send, part_recv, slope, rg, rg_out, lg_all,
+    look, look_in, part_send, part_recv, slope, rg, rg_out, lg_col, lg_all,
     lsem, osem, ssem, rsem,
 ):
-    S = cols.shape[0]
-    F = cols.shape[1] // 2
+    F, S = now_t.shape
     R, W = tab.shape
     H = bias.shape[1]
     FW = F * W
-    half = S // 2
-    nb = M // 2
-    B = half // nb
+    part = S // TEAM
+    nb = M // TEAM
+    B = part // nb
     slots = D * C
     rsh, csh = log2(R), log2(C)
     dp, mp = lax.axis_index("dp"), lax.axis_index("mp")
     me = dp * M + mp
-    h = lax.rem(mp, 2)
-    myb = lax.div(mp, 2)
-    partner = (dp, mp + 1 - 2 * h)
+    g = lax.rem(mp, TEAM)
+    myb = lax.div(mp, TEAM)
+    core = lax.rem(dp, 2)
+    sibling = (dp + 1 - 2 * core, mp)
+
+    def mate(k):
+        return (dp, myb * TEAM + lax.rem(g + k, TEAM))
+
+    def twin(k):
+        return (dp, lax.rem(myb + k, nb) * TEAM + g)
+
+    partner = mate(1)
 
     def device(p):
         return (lax.div(p, M), lax.rem(p, M))
@@ -87,6 +96,13 @@
         lax.broadcasted_iota(jnp.int32, (S, S), 0)
         > lax.broadcasted_iota(jnp.int32, (S, S), 1)
     )
+    sub = lax.broadcasted_iota(jnp.int32, (128, S), 0)
+    stacked = jnp.zeros((128, S), F32)
+    for q in range(2 * F + 1):
+        line = labels_t[...] if q == 2 * F else (now_t, later_t)[q // F][q % F : q % F + 1, :]
+        stacked = jnp.where(sub == q, line.astype(F32), stacked)
+    colscr[...] = stacked.T
+    cols = colscr[...].astype(jnp.int32)
     owners, members = [], []
     for q in range(2 * F):
         owner = (lax.shift_right_logical(cols[:, q : q + 1], rsh) - me) & (D - 1)
@@ -102,6 +118,7 @@
         rank = jnp.sum(count * members[q], axis=1, keepdims=True).astype(jnp.int32)
         ranks.append(rank)
         packed = jnp.where(lane == q, (owners[q] * C + rank).astype(F32), packed)
+    slotcol[...] = packed.astype(jnp.int32)
     rowscr[...] = packed.T[0:8, :].astype(jnp.int32)
     total = jnp.zeros((D, 256), F32)
     owner_iota = lax.broadcasted_iota(jnp.int32, (D, S), 0)
@@ -139,8 +156,12 @@
     exchange(8, req_send, asked, 0, 1, D)
     asked[0:8, :] = req_send[0:8, :]
     loads[1].wait()
-    copy_w = remote(w.at[0], w.at[1], 1, partner)
-    copy_w.start()
+    share = pl.ds(pl.multiple_of(core * (FW // 2), FW // 2), FW // 2)
+    for k in range(1, TEAM):
+        remote(w.at[0, share], w.at[TEAM - k, share], 1, mate(k)).start()
+    others = w.at[pl.ds(1, TEAM - 1), share]
+    copy_w = remote(others, others, 1, partner)
+    pass_w = remote(others, others, 12, sibling)
     loads[0].wait()
     tabh[...] = tab[...].astype(BF16)
     copy_req = arrived(8, req_send, asked, 0)
@@ -156,8 +177,8 @@
     KC = 1024
 
     def fetch(t, source, send, recv, n):
-        def group(g, c):
-            rows = pl.ds(pl.multiple_of(g * GROUP, GROUP), GROUP)
+        def group(i, c):
+            rows = pl.ds(pl.multiple_of(i * GROUP, GROUP), GROUP)
             ids = idcol[t, rows, 0:1]
             acc = jnp.zeros((GROUP, W), F32)
             for k in range(R // KC):
@@ -167,40 +188,52 @@
                 acc = acc + mm(pick, source[k * KC : (k + 1) * KC, :])
             send[rows, :] = acc.astype(BF16)
             peers = GROUP // C
-            exchange(C, send, recv, n, jnp.maximum(g * peers, 1), (g + 1) * peers)
+            exchange(C, send, recv, n, jnp.maximum(i * peers, 1), (i + 1) * peers)
             return c
 
         lax.fori_loop(0, slots // GROUP, group, 0)
         recv[0:C, :] = send[0:C, :]
 
     def forward(t, recv, n):
-        for f in range(F):
-            owner_rank = jnp.broadcast_to(slot_col[t * F + f], (S, slots))
-            pick = onehot(owner_rank == lax.broadcasted_iota(jnp.int32, (S, slots), 1))
+        def look_up(k):
+            rows = pl.ds(pl.multiple_of(lax.rem(g + k, TEAM) * part, part), part)
+            slot = jnp.concatenate(
+                [slotcol[rows, t * F + f : t * F + f + 1] for f in range(F)], axis=0
+            )
+            pick = onehot(slot == lax.broadcasted_iota(jnp.int32, (F * part, slots), 1))
             got = mm(pick, recv[...]).astype(BF16)
-            look[t, 0, :, f * W : (f + 1) * W] = got[:half]
-            look[t, 1, :, f * W : (f + 1) * W] = got[half:]
-        swap = remote(look.at[t, 1 - h], look.at[t, 2], n, partner)
-        swap.start()
+            for f in range(F):
+                look[t, k, :, f * W : (f + 1) * W] = got[f * part : (f + 1) * part]
+
+        for k in range(1, TEAM):
+            look_up(k)
+            remote(look.at[t, k], look_in.at[t, TEAM - k], n, mate(k)).start()
+        look_up(0)
+        look_in[t, 0] = look[t, 0]
+        swap = remote(
+            look.at[t, pl.ds(1, TEAM - 1)], look_in.at[t, pl.ds(1, TEAM - 1)], n, partner
+        )
         if t == 0:
-            copy_w.wait_recv()
+            pass_w.wait_recv()
         swap.wait_recv()
+
+        def layer(rows):
+            value = mm(look_in[t, 0, rows, :], w[0])
+            for k in range(1, TEAM):
+                value = value + mm(look_in[t, k, rows, :], w[k])
+            return value
 
         def step(i, c):
             k = i + 1
             b = lax.rem(myb + k, nb)
             rows = pl.ds(pl.multiple_of(b * B, B), B)
-            value = mm(look[t, h, rows, :], w[0]) + mm(look[t, 2, rows, :], w[1])
-            part_send[t, k] = value.astype(BF16)
-            remote(
-                part_send.at[t, k], part_recv.at[t, nb - k], n + 1, (dp, 2 * b + h)
-            ).start()
+            part_send[t, k] = layer(rows).astype(BF16)
+            remote(part_send.at[t, k], part_recv.at[t, nb - k], n + 1, twin(k)).start()
             return c
 
         lax.fori_loop(0, nb - 1, step, 0)
         rows = pl.ds(pl.multiple_of(myb * B, B), B)
-        pre = mm(look[t, h, rows, :], w[0]) + mm(look[t, 2, rows, :], w[1])
-        pre = pre + bias[...]
+        pre = layer(rows) + bias[...]
         moved = remote(
             part_send.at[t, pl.ds(1, nb - 1)], part_recv.at[t, pl.ds(1, nb - 1)],
             n + 1, partner,
@@ -212,57 +245,67 @@
         logits = jnp.sum(pre * gate * wout[...], axis=1, keepdims=True)
         return pre, gate, logits, [swap, moved]
 
-    slot_col = [owners[q] * C + ranks[q] for q in range(2 * F)]
     fetch(0, tabh, send_now, recv_now, 2)
     for blk in range(slots // 128):
         flipped = idcol[0, blk * 128 : (blk + 1) * 128, :].astype(F32).T
         idrow[:, blk * 128 : (blk + 1) * 128] = flipped[0:8, :].astype(jnp.int32)
+    copy_w.wait_recv()
+    pass_w.start()
+
+    RC = 256
+
+    def mark(i, c):
+        rows = pl.ds(pl.multiple_of(i * RC, RC), RC)
+        spot = lax.broadcasted_iota(jnp.int32, (RC, slots), 0) + i * RC
+        scatter[rows, :] = onehot(idrow[0:1, :] == spot)
+        return c
+
+    lax.fori_loop(0, R // RC, mark, 0)
     copy_now = arrived(C, send_now, recv_now, 2)
     copy_now.wait_recv()
     pre, gate, logits, sent_now = forward(0, recv_now, 3)
-    mine = pl.ds(pl.multiple_of(h * half + myb * B, B), B)
-    error = jax.nn.sigmoid(logits) - labels[mine, :].astype(F32)
+    mine = pl.ds(pl.multiple_of(g * part + myb * B, B), B)
+    error = jax.nn.sigmoid(logits) - colscr[mine, 2 * F : 2 * F + 1]
     slope[0] = (error * wout[...] * (gate * (1.0 + pre * (1.0 - gate)))).astype(BF16)
 
     def spread(k, c):
-        remote(
-            slope.at[0], slope.at[nb - k], 5, (dp, 2 * lax.rem(myb + k, nb) + h)
-        ).start()
+        remote(slope.at[0], slope.at[nb - k], 5, twin(k)).start()
         return c
 
     lax.fori_loop(1, nb, spread, 0)
 
     def back(k):
         rows = pl.ds(pl.multiple_of(lax.rem(myb + k, nb) * B, B), B)
-        for side in range(2):
+        for side in range(TEAM):
             value = lax.dot_general(
                 slope[k], w[side], (((1,), (1,)), ((), ())), preferred_element_type=F32
             ).astype(BF16)
-            if side == 0:
-                rg[h, rows, :] = value
-            else:
-                rg_out[rows, :] = value
+            rg_out[side, rows, :] = value
 
     back(0)
     copy_slope = remote(slope.at[pl.ds(1, nb - 1)], slope.at[pl.ds(1, nb - 1)], 5, partner)
     copy_slope.wait_recv()
     for k in range(1, nb):
         back(k)
-    swap_grad = remote(rg_out, rg.at[h], 6, partner)
-    swap_grad.start()
+    for k in range(1, TEAM):
+        remote(rg_out.at[k], rg.at[g], 6, mate(k)).start()
+    rg[g] = rg_out[0]
+    swap_grad = remote(
+        rg_out.at[pl.ds(1, TEAM - 1)], rg.at[pl.ds(1, TEAM - 1)], 6, partner
+    )
     swap_grad.wait_recv()
-
-    def give(g, c):
-        rows = pl.ds(pl.multiple_of(g * GROUP, GROUP), GROUP)
+    grads = rg[...].reshape(S, FW)
+
+    def give(i, c):
+        rows = pl.ds(pl.multiple_of(i * GROUP, GROUP), GROUP)
         acc = jnp.zeros((GROUP, W), F32)
-        spot = lax.broadcasted_iota(jnp.int32, (GROUP, half), 0) + g * GROUP
+        spot = lax.broadcasted_iota(jnp.int32, (GROUP, S), 0) + i * GROUP
         for f in range(F):
-            for s in range(2):
-                pick = onehot(rowscr[f : f + 1, s * half : (s + 1) * half] == spot)
-                acc = acc + mm(pick, rg[s, :, f * W : (f + 1) * W])
+            pick = onehot(rowscr[f : f + 1, :] == spot)
+            acc = acc + mm(pick, grads[:, f * W : (f + 1) * W])
         send_grad[rows, :] = acc.astype(BF16)
         peers = GROUP // C
-        exchange(C, send_grad, recv_grad, 7, jnp.maximum(g * peers, 1), (g + 1) * peers)
+        exchange(C, send_grad, recv_grad, 7, jnp.maximum(i * peers, 1), (i + 1) * peers)
         return c
 
     lax.fori_loop(0, slots // GROUP, give, 0)
@@ -272,18 +315,16 @@
     copy_grad = arrived(C, send_grad, recv_grad, 7)
     copy_grad.wait_recv()
 
-    RC = 256
     gathered = jnp.concatenate([recv_grad[...], jnp.ones((slots, 128), BF16)], axis=1)
 
     def update(i, c):
         rows = pl.ds(pl.multiple_of(i * RC, RC), RC)
-        spot = lax.broadcasted_iota(jnp.int32, (RC, slots), 0) + i * RC
-        both = mm(onehot(idrow[0:1, :] == spot), gathered)
-        g, keep = both[:, :W], both[:, W:] > 0.5
+        both = mm(scatter[rows, :], gathered)
+        grad, keep = both[:, :W], both[:, W:] > 0.5
         old_w, old_d, old_s = tab[rows, :], dual[rows, :], sq[rows, :]
-        new_s = old_s + g * g
+        new_s = old_s + grad * grad
         root = jnp.sqrt(new_s)
-        new_d = old_d + g - (root - jnp.sqrt(old_s)) * old_w
+        new_d = old_d + grad - (root - jnp.sqrt(old_s)) * old_w
         shrunk = jnp.where(new_d > 0.0, new_d - LASSO, new_d + LASSO)
         new_w = jnp.where(
             jnp.abs(new_d) <= LASSO, 0.0, -shrunk / ((BETA + root) + RIDGE)
@@ -308,17 +349,16 @@
     copy_next = arrived(C, send_next, recv_next, 8)
     copy_next.wait_recv()
     pre, gate, logits, sent_next = forward(1, recv_next, 9)
-    wide = jnp.broadcast_to(logits, (B, 128))
-    if B < 128:
-        wide = jnp.concatenate([wide, jnp.zeros((128 - B, 128), F32)], axis=0)
-    lg_all[mp] = wide.T[0:8, :]
+    lg_col[...] = jnp.zeros((128, 128), F32)
+    lg_col[pl.ds(pl.multiple_of(myb * B, B), B), :] = jnp.broadcast_to(logits, (B, 128))
+    lg_all[mp] = lg_col[...].T[0:8, :]
 
     def tell(k, c):
         remote(lg_all.at[mp], lg_all.at[mp], 11, (dp, lax.rem(mp + k, M))).start()
         return c
 
     lax.fori_loop(1, M, tell, 0)
-    for copy in (copy_req, copy_w, copy_now, *sent_now, copy_slope, swap_grad, copy_grad,
+    for copy in (copy_req, copy_w, pass_w, copy_now, *sent_now, copy_slope, swap_grad, copy_grad,
                  copy_next, *sent_next):
         copy.wait_send()
     for store in stores:
@@ -326,7 +366,11 @@
     told = remote(lg_all.at[pl.ds(0, M - 1)], lg_all.at[pl.ds(0, M - 1)], 11, partner)
     told.wait_send()
     told.wait_recv()
-    lg_o[...] = lg_all[...]
+    for k in range(TEAM):
+        line = lg_all[k]
+        for b in range(1, nb):
+            line = line + lg_all[b * TEAM + k]
+        lg_o[k : k + 1, :] = line[0:1, :]
 
 
 def shards(table, dual, squares, now, later, labels, weight, bias, wout):
@@ -338,8 +382,7 @@
     C = 2 * now.size // D
     slots = D * C
     GROUP = 512
-    nb = M // 2
-    B = S // M
+    part, nb, B = S // TEAM, M // TEAM, S // M
     vm = pl.BlockSpec(memory_space=pltpu.VMEM)
     hb = pl.BlockSpec(memory_space=pl.ANY)
     rows_buf = pltpu.VMEM((slots, W), BF16)
@@ -347,33 +390,34 @@
     state = jax.ShapeDtypeStruct((R, W), F32)
     outs = pl.pallas_call(
         functools.partial(train, D, M, C, GROUP),
-        out_shape=(state, state, state, jax.ShapeDtypeStruct((M, 8, 128), F32)),
-        in_specs=[vm, vm, vm, vm, hb, hb, hb, hb],
+        out_shape=(state, state, state, jax.ShapeDtypeStruct((TEAM, 128), F32)),
+        in_specs=[vm, vm, vm, vm, vm, hb, hb, hb, hb],
         out_specs=(hb, hb, hb, vm),
         scratch_shapes=[
             big, big, big,
             pltpu.VMEM((R, W), BF16), pltpu.VMEM((R, W), BF16),
-            pltpu.VMEM((2, F * W, H), BF16),
+            pltpu.VMEM((TEAM, F * W, H), BF16), pltpu.VMEM((R, slots), BF16),
+            pltpu.VMEM((S, 128), F32), pltpu.VMEM((S, 128), jnp.int32),
             pltpu.VMEM((8, S), jnp.int32),
             pltpu.VMEM((D * 8, 128), jnp.int32), pltpu.VMEM((D * 8, 128), jnp.int32),
             pltpu.VMEM((2, slots, 128), jnp.int32), pltpu.VMEM((8, slots), jnp.int32),
             rows_buf, rows_buf, rows_buf, rows_buf, rows_buf, rows_buf,
-            pltpu.VMEM((2, 3, S // 2, F * W), BF16),
+            pltpu.VMEM((2, TEAM, part, F * W), BF16), pltpu.VMEM((2, TEAM, part, F * W), BF16),
             pltpu.VMEM((2, nb, B, H), BF16), pltpu.VMEM((2, nb, B, H), BF16),
             pltpu.VMEM((nb, B, H), BF16),
-            pltpu.VMEM((2, S // 2, F * W), BF16), pltpu.VMEM((S // 2, F * W), BF16),
-            pltpu.VMEM((M, 8, 128), F32),
+            pltpu.VMEM((TEAM, part, F * W), BF16), pltpu.VMEM((TEAM, part, F * W), BF16),
+            pltpu.VMEM((128, 128), F32), pltpu.VMEM((M, 8, 128), F32),
             pltpu.SemaphoreType.DMA((4,)), pltpu.SemaphoreType.DMA((3,)),
-            pltpu.SemaphoreType.DMA((12,)), pltpu.SemaphoreType.DMA((12,)),
+            pltpu.SemaphoreType.DMA((13,)), pltpu.SemaphoreType.DMA((13,)),
         ],
         compiler_params=pltpu.CompilerParams(
             collective_id=0, has_side_effects=True, vmem_limit_bytes=58 * 1024 * 1024
         ),
     )(
-        jnp.concatenate([now, later], axis=1), labels[:, None], bias[None, :],
-        wout[None, :], table, dual, squares, weight,
+        now.T, later.T, labels[None, :], bias[None, :], wout[None, :],
+        table, dual, squares, weight,
     )
-    logits = outs[3][:, 0, :B].reshape(nb, 2, B).transpose(1, 0, 2).reshape(S)
+    logits = outs[3].reshape(S)
     return outs[0], outs[1], outs[2], logits
 
 

time: 138 us -> 122 us (0.88)
  Pallas kernels: 125 us -> 113 us
  local copies, waits for them, and re-layouts: 10.7 us -> 7.45 us
    pallas_call x1, Pallas kernels: 125 us -> 113 us  [shards(): pl.pallas_call(functools.partial(train, D, M, C, GROUP), out_shape=(state...]
    broadcast_in_dim x1 -> x0, local copies, waits for them, and re-layouts: 1.53 us -> none  [shards(): labels[:, None]]
    unnamed x7 -> x10, local copies, waits for them, and re-layouts: 6.86 us -> 7.45 us
where the time goes in v2:
time: 122 us; the launch traced here: 121 us
  Pallas kernels  113 us (93%)
  local copies, waits for them, and re-layouts  7.45 us (6%)
    pallas_call x1, Pallas kernels, shards(): pl.pallas_call(functools.partial(train, D, M, C, GROUP), out_shape=(state...  113 us
    unnamed x10, local copies, waits for them, and re-layouts  7.45 us

profile of v2, /device:TPU:0, one launch (start us, length us, event | category | flops | bytes accessed | tf_op | source)
XLA Modules:
  0.0 121.4 jit_solution(12755482059926707668)
XLA Ops:
  0.6 113.3 %shard_map.120 = (f32[4096,128]{1,0:T(8,128)}, f32[4096,128]{1,0:T(8,128)}, f32[4096,128]{1,0:T(8,128)}, f32[4,128]{1,0:T(4,128)}) custom-call(s32[2,512]{1,0:T(2,128)} %bitcast.6, s32[2,512]{1,0:T(2,128)} %bitcast.7, s32[1,512]{1,0:T(1,128)} %bitcast.10, f32[1,1024]{1,0:T(1,128)} %bitcast.8, f32[1,1024]{1,0:T(1,128)} %bitcast.9, f32[4096,128]{1,0:T(8,128)} %table_h.1, ...), custom_call_target="tpu_custom_call" | custom-call | tf_op jit(solution)/shard_map/pallas_call | solution.py:391
  113.9 0.0 copy-start.1
  113.9 3.2 %copy.17 = f32[4096,128]{1,0:T(8,128)} copy(f32[4096,128]{1,0:T(8,128)} %get-tuple-element.16) | data formatting | bytes 4194304
  117.1 0.0 copy-done.1
  117.1 0.0 copy-start
  117.1 1.3 %copy.18 = f32[4096,128]{1,0:T(8,128)} copy(f32[4096,128]{1,0:T(8,128)S(1)} %copy-done.1) | data formatting | bytes 4194304
  118.4 1.0 copy-done
  119.5 0.0 copy-start.2
  119.5 1.3 %copy.19 = f32[4096,128]{1,0:T(8,128)} copy(f32[4096,128]{1,0:T(8,128)S(1)} %copy-done) | data formatting | bytes 4194304
  120.8 0.0 copy-done.2
  120.8 0.6 copy.20
Async XLA Ops:
  113.9 3.2 %copy-start.1 = (f32[4096,128]{1,0:T(8,128)S(1)}, f32[4096,128]{1,0:T(8,128)}, u32[]{:S(2)}) copy-start(f32[4096,128]{1,0:T(8,128)} %get-tuple-element.17) | copy-start | bytes 6291460
  117.1 2.3 %copy-start = (f32[4096,128]{1,0:T(8,128)S(1)}, f32[4096,128]{1,0:T(8,128)}, u32[]{:S(2)}) copy-start(f32[4096,128]{1,0:T(8,128)} %get-tuple-element.18) | copy-start | bytes 6291460
  119.5 1.3 %copy-start.2 = (f32[4,128]{1,0:T(4,128)S(1)}, f32[4,128]{1,0:T(4,128)}, u32[]{:S(2)}) copy-start(f32[4,128]{1,0:T(4,128)} %get-tuple-element.11) | copy-start | bytes 6148

commit v3 on v2

--- a/solution.py
+++ b/solution.py
@@ -53,7 +53,9 @@
     g = lax.rem(mp, TEAM)
     myb = lax.div(mp, TEAM)
     core = lax.rem(dp, 2)
+    side = lax.rem(lax.div(dp, 2), 2)
     sibling = (dp + 1 - 2 * core, mp)
+    across = (dp + 2 - 4 * side, mp)
 
     def mate(k):
         return (dp, myb * TEAM + lax.rem(g + k, TEAM))
@@ -64,13 +66,13 @@
     partner = mate(1)
 
     def device(p):
-        return (lax.div(p, M), lax.rem(p, M))
+        return (lax.shift_right_logical(p, log2(M)), p & (M - 1))
 
     bar = pltpu.get_barrier_semaphore()
 
     def greet(k, c):
         pl.semaphore_signal(
-            bar, inc=1, device_id=device(lax.rem(me + k, D)), device_id_type=MESH
+            bar, inc=1, device_id=device((me + k) & (D - 1)), device_id_type=MESH
         )
         return c
 
@@ -143,7 +145,7 @@
             remote(
                 send.at[pl.ds(pl.multiple_of(r * rows, rows), rows)],
                 recv.at[pl.ds(pl.multiple_of((D - r) * rows, rows), rows)],
-                n, device(lax.rem(me + r, D)),
+                n, device((me + r) & (D - 1)),
             ).start()
             return c
 
@@ -156,12 +158,16 @@
     exchange(8, req_send, asked, 0, 1, D)
     asked[0:8, :] = req_send[0:8, :]
     loads[1].wait()
-    share = pl.ds(pl.multiple_of(core * (FW // 2), FW // 2), FW // 2)
+    quarter = pl.ds(pl.multiple_of((2 * core + side) * (FW // 4), FW // 4), FW // 4)
     for k in range(1, TEAM):
-        remote(w.at[0, share], w.at[TEAM - k, share], 1, mate(k)).start()
-    others = w.at[pl.ds(1, TEAM - 1), share]
-    copy_w = remote(others, others, 1, partner)
-    pass_w = remote(others, others, 12, sibling)
+        remote(w.at[0, quarter], w.at[TEAM - k, quarter], 1, mate(k)).start()
+    share = w.at[pl.ds(1, TEAM - 1), quarter]
+    copy_w = remote(share, share, 1, partner)
+    cross_w = remote(share, share, 13, across)
+    both = w.at[
+        pl.ds(1, TEAM - 1), pl.ds(pl.multiple_of(core * (FW // 2), FW // 2), FW // 2)
+    ]
+    pass_w = remote(both, both, 12, sibling)
     loads[0].wait()
     tabh[...] = tab[...].astype(BF16)
     copy_req = arrived(8, req_send, asked, 0)
@@ -245,14 +251,16 @@
         logits = jnp.sum(pre * gate * wout[...], axis=1, keepdims=True)
         return pre, gate, logits, [swap, moved]
 
+    copy_w.wait_recv()
+    cross_w.start()
     fetch(0, tabh, send_now, recv_now, 2)
     for blk in range(slots // 128):
         flipped = idcol[0, blk * 128 : (blk + 1) * 128, :].astype(F32).T
         idrow[:, blk * 128 : (blk + 1) * 128] = flipped[0:8, :].astype(jnp.int32)
-    copy_w.wait_recv()
+    cross_w.wait_recv()
     pass_w.start()
 
-    RC = 256
+    RC = 1024
 
     def mark(i, c):
         rows = pl.ds(pl.multiple_of(i * RC, RC), RC)
@@ -358,7 +366,7 @@
         return c
 
     lax.fori_loop(1, M, tell, 0)
-    for copy in (copy_req, copy_w, pass_w, copy_now, *sent_now, copy_slope, swap_grad, copy_grad,
+    for copy in (copy_req, copy_w, cross_w, pass_w, copy_now, *sent_now, copy_slope, swap_grad, copy_grad,
                  copy_next, *sent_next):
         copy.wait_send()
     for store in stores:
@@ -381,7 +389,7 @@
     H = weight.shape[1]
     C = 2 * now.size // D
     slots = D * C
-    GROUP = 512
+    GROUP = 256
     part, nb, B = S // TEAM, M // TEAM, S // M
     vm = pl.BlockSpec(memory_space=pltpu.VMEM)
     hb = pl.BlockSpec(memory_space=pl.ANY)
@@ -408,7 +416,7 @@
             pltpu.VMEM((TEAM, part, F * W), BF16), pltpu.VMEM((TEAM, part, F * W), BF16),
             pltpu.VMEM((128, 128), F32), pltpu.VMEM((M, 8, 128), F32),
             pltpu.SemaphoreType.DMA((4,)), pltpu.SemaphoreType.DMA((3,)),
-            pltpu.SemaphoreType.DMA((13,)), pltpu.SemaphoreType.DMA((13,)),
+            pltpu.SemaphoreType.DMA((14,)), pltpu.SemaphoreType.DMA((14,)),
         ],
         compiler_params=pltpu.CompilerParams(
             collective_id=0, has_side_effects=True, vmem_limit_bytes=58 * 1024 * 1024

time: 122 us -> 118 us (0.967)
  Pallas kernels: 113 us -> 110 us
    pallas_call x1, Pallas kernels: 113 us -> 110 us  [shards(): pl.pallas_call(functools.partial(train, D, M, C, GROUP), out_shape=(state...]
where the time goes in v3:
time: 118 us
  Pallas kernels  110 us (93%)
  local copies, waits for them, and re-layouts  7.45 us (6%)
    pallas_call x1, Pallas kernels, shards(): pl.pallas_call(functools.partial(train, D, M, C, GROUP), out_shape=(state...  110 us
    unnamed x10, local copies, waits for them, and re-layouts  7.45 us

profile of v3, /device:TPU:0, one launch (start us, length us, event | category | flops | bytes accessed | tf_op | source)
XLA Modules:
  0.0 117.7 jit_solution(165915216859363098)
XLA Ops:
  0.6 109.6 %shard_map.120 = (f32[4096,128]{1,0:T(8,128)}, f32[4096,128]{1,0:T(8,128)}, f32[4096,128]{1,0:T(8,128)}, f32[4,128]{1,0:T(4,128)}) custom-call(s32[2,512]{1,0:T(2,128)} %bitcast.6, s32[2,512]{1,0:T(2,128)} %bitcast.7, s32[1,512]{1,0:T(1,128)} %bitcast.10, f32[1,1024]{1,0:T(1,128)} %bitcast.8, f32[1,1024]{1,0:T(1,128)} %bitcast.9, f32[4096,128]{1,0:T(8,128)} %table_h.1, ...), custom_call_target="tpu_custom_call" | custom-call | tf_op jit(solution)/shard_map/pallas_call | solution.py:399
  110.3 0.0 copy-start.1
  110.3 3.2 %copy.17 = f32[4096,128]{1,0:T(8,128)} copy(f32[4096,128]{1,0:T(8,128)} %get-tuple-element.16) | data formatting | bytes 4194304
  113.5 0.0 copy-done.1
  113.5 0.0 copy-start
  113.5 1.3 %copy.18 = f32[4096,128]{1,0:T(8,128)} copy(f32[4096,128]{1,0:T(8,128)S(1)} %copy-done.1) | data formatting | bytes 4194304
  114.8 1.0 copy-done
  115.8 0.0 copy-start.2
  115.8 1.3 %copy.19 = f32[4096,128]{1,0:T(8,128)} copy(f32[4096,128]{1,0:T(8,128)S(1)} %copy-done) | data formatting | bytes 4194304
  117.1 0.0 copy-done.2
  117.1 0.6 copy.20
Async XLA Ops:
  110.3 3.2 %copy-start.1 = (f32[4096,128]{1,0:T(8,128)S(1)}, f32[4096,128]{1,0:T(8,128)}, u32[]{:S(2)}) copy-start(f32[4096,128]{1,0:T(8,128)} %get-tuple-element.17) | copy-start | bytes 6291460
  113.5 2.3 %copy-start = (f32[4096,128]{1,0:T(8,128)S(1)}, f32[4096,128]{1,0:T(8,128)}, u32[]{:S(2)}) copy-start(f32[4096,128]{1,0:T(8,128)} %get-tuple-element.18) | copy-start | bytes 6291460
  115.8 1.3 %copy-start.2 = (f32[4,128]{1,0:T(4,128)S(1)}, f32[4,128]{1,0:T(4,128)}, u32[]{:S(2)}) copy-start(f32[4,128]{1,0:T(4,128)} %get-tuple-element.11) | copy-start | bytes 6148
